TPU v7x, 256 devices: a whole 4x4x8 slice. The times are simulated.
256 devices in a mesh: dp: 8 (over x, core), seq: 32 (over z, y).
Axes of the slice: x: 4, y: 4, z: 8, core: 2. Of those that a mesh axis runs over, the one named last changes fastest.
Arguments:
- queries: bfloat16 [8, 32, 512, 512], P('dp', 'seq'), may hold values from -8 to 8
- keys: bfloat16 [8, 32, 512, 128], P('dp', 'seq'), may hold values from -8 to 8
- values: bfloat16 [8, 32, 512, 128], P('dp', 'seq'), may hold values from -6 to 6
- grad_out: bfloat16 [8, 32, 512, 4096], P('dp', 'seq'), may hold values from -6 to 6
- out_weight: bfloat16 [4096, 512], P('dp'), may hold values from -0.25 to 0.25
- ancestors: int32 [8, 32, 3], P('dp'), may hold values from -1 to 30, as said below
- owner: int32 [8, 32], P('dp'), may hold values from 0 to 31, each once within a row
- lengths: int32 [8, 32], P('dp'), may hold values from 128 to 512, as said below
Outputs:
- grad_queries: bfloat16 [8, 32, 512, 512], P('dp', 'seq')
- grad_keys: bfloat16 [8, 32, 512, 128], P('dp', 'seq')
- grad_values: bfloat16 [8, 32, 512, 128], P('dp', 'seq')
- grad_weight: float32 [4096, 512], P(('dp', 'seq'))
Inputs may be any that keep to these rules, and one draw needn't show every extreme that they name: Row n lists node n's ancestors root first, each the parent of the next and the last the parent of n, then -1 in the places left; every ancestor has a smaller id than n; node 0 is the root of each pack and has none; some node has exactly 3. `lengths`: the used tokens are the first ones of the tile; the root's tile is full.
All inputs are finite; a program needn't handle non-finite values.
Results may differ from a plain program's by a relative error of at most 0.023.
Values may be sent and summed in bfloat16 or wider, within the bound.
No kernel may reach another device: no remote copies, remote signals or barrier semaphores. Data moves between devices by JAX's collectives and lax.ppermute only.
A program may use at most 128 MiB of HBM per device.

v0:
```python
import math

import jax
import jax.numpy as jnp
from jax import lax
from jax.sharding import PartitionSpec as P

MASKED = -1e30


def slot_tables(ancestor_table, owner_row, length_row):
    node_count = owner_row.shape[0]
    node_ids = jnp.arange(node_count, dtype=jnp.int32)
    matches = owner_row[:, None] == node_ids[None, :]
    tile_length = jnp.sum(jnp.where(matches, length_row[:, None], 0), axis=0)
    ancestor_nodes = jnp.sum(jnp.where(matches[:, :, None], ancestor_table[:, None, :], 0), axis=0)
    ancestor_hits = ancestor_nodes[:, :, None] == node_ids[None, None, :]
    ancestor_slots = jnp.sum(jnp.where(ancestor_hits, owner_row[None, None, :], 0), axis=2)
    ancestor_slots = jnp.where(ancestor_nodes >= 0, ancestor_slots, -1)
    key_slots = jnp.concatenate([ancestor_slots, node_ids[:, None]], axis=1)
    return (key_slots, tile_length)


def key_visible(key_length, self_tile, tile_size):
    query_pos = lax.broadcasted_iota(jnp.int32, (tile_size, tile_size), 0)
    key_pos = lax.broadcasted_iota(jnp.int32, (tile_size, tile_size), 1)
    return (key_pos < key_length) & ((key_pos <= query_pos) | jnp.logical_not(self_tile))


def per_device(queries, keys, values, grad_out, out_weight, ancestors, owner, lengths):
    local_queries = queries[0]
    tile_count, tile_rows, query_width = local_queries.shape
    head_width = keys.shape[-1]
    head_count = query_width // head_width
    ancestor_depth = ancestors.shape[-1]
    score_scale = 1.0 / math.sqrt(head_width)
    key_slots, tile_length = slot_tables(ancestors[0], owner[0], lengths[0])
    first_slot = lax.axis_index("seq") * tile_count
    local_length = lax.dynamic_slice_in_dim(tile_length, first_slot, tile_count)
    local_slots = lax.dynamic_slice_in_dim(key_slots, first_slot, tile_count)
    key_values = jnp.concatenate([keys[0], values[0]], axis=-1)
    pack_tiles = lax.all_gather(key_values, "seq", axis=0, tiled=True)
    positions = lax.broadcasted_iota(jnp.int32, (tile_count, tile_rows), 1)
    masked_grads = jnp.where(
        (positions < local_length[:, None])[..., None], grad_out[0], jnp.zeros((), jnp.bfloat16)
    )
    flat_grads = masked_grads.reshape(tile_count * tile_rows, -1)
    columns = flat_grads
    grad_attn_all = jnp.dot(
        columns,
        lax.all_gather(out_weight, "dp", axis=0, tiled=True),
        preferred_element_type=jnp.float32,
    ).astype(jnp.bfloat16)
    grad_attn_all = grad_attn_all.reshape(tile_count, tile_rows, head_count, head_width)
    shaped_queries = local_queries.reshape(tile_count, tile_rows, head_count, head_width)
    step_order = jnp.arange(ancestor_depth + 1, dtype=jnp.int32)

    def tile_pass(key_buffer, tile_index):
        tile_query = lax.dynamic_index_in_dim(shaped_queries, tile_index, 0, keepdims=False)
        grad_attn = lax.dynamic_index_in_dim(grad_attn_all, tile_index, 0, keepdims=False)
        tile_slots = lax.dynamic_index_in_dim(local_slots, tile_index, 0, keepdims=False)

        def logits(step_index):
            safe_slot = jnp.maximum(tile_slots[step_index], 0)
            kv_tile = lax.dynamic_index_in_dim(pack_tiles, safe_slot, 0, keepdims=False)
            key_part = kv_tile[:, :head_width]
            value_part = kv_tile[:, head_width:]
            visible = key_visible(tile_length[safe_slot], step_index == ancestor_depth, tile_rows)
            scores = (
                jnp.einsum("qhd,kd->qhk", tile_query, key_part, preferred_element_type=jnp.float32)
                * score_scale
            )
            return (
                jnp.where(visible[:, None, :], scores, MASKED),
                visible,
                key_part,
                value_part,
                safe_slot,
            )

        def forward(carried, step_index):

            def forward_take_tile(forward_state):
                row_max, row_total, weighted = forward_state
                scores, visible, key_part, value_part, safe_slot = logits(step_index)
                new_max = jnp.maximum(row_max, jnp.max(scores, axis=2))
                weights = jnp.where(visible[:, None, :], jnp.exp(scores - new_max[..., None]), 0.0)
                factor = jnp.exp(row_max - new_max)
                product = jnp.einsum(
                    "qhk,kd->qhd",
                    weights.astype(jnp.bfloat16),
                    value_part,
                    preferred_element_type=jnp.float32,
                )
                return (
                    new_max,
                    row_total * factor + jnp.sum(weights, axis=2),
                    weighted * factor[..., None] + product,
                )

            return (
                lax.cond(
                    tile_slots[step_index] >= 0,
                    forward_take_tile,
                    lambda forward_state: forward_state,
                    carried,
                ),
                None,
            )

        initial = (
            jnp.full((tile_rows, head_count), MASKED, jnp.float32),
            jnp.zeros((tile_rows, head_count), jnp.float32),
            jnp.zeros((tile_rows, head_count, head_width), jnp.float32),
        )
        (row_max, row_total, weighted), _ = lax.scan(forward, initial, step_order)
        attention = weighted / row_total[..., None]
        log_total = row_max + jnp.log(row_total)
        row_delta = jnp.sum(grad_attn.astype(jnp.float32) * attention, axis=-1)

        def backward(back_state, step_index):

            def backward_take_tile(inner_state):
                grad_query, buffer_now = inner_state
                scores, visible, key_part, value_part, safe_slot = logits(step_index)
                probabilities = jnp.where(
                    visible[:, None, :], jnp.exp(scores - log_total[..., None]), 0.0
                )
                probs_low = probabilities.astype(jnp.bfloat16)
                grad_probs = jnp.einsum(
                    "qhd,kd->qhk", grad_attn, value_part, preferred_element_type=jnp.float32
                )
                grad_scores = (
                    probabilities * (grad_probs - row_delta[..., None]) * score_scale
                ).astype(jnp.bfloat16)
                grad_query = grad_query + jnp.einsum(
                    "qhk,kd->qhd", grad_scores, key_part, preferred_element_type=jnp.float32
                )
                grad_key_part = jnp.einsum(
                    "qhk,qhd->kd", grad_scores, tile_query, preferred_element_type=jnp.float32
                )
                grad_value_part = jnp.einsum(
                    "qhk,qhd->kd", probs_low, grad_attn, preferred_element_type=jnp.float32
                )
                previous = lax.dynamic_index_in_dim(buffer_now, safe_slot, 0, keepdims=False)
                updated = previous + jnp.concatenate([grad_key_part, grad_value_part], axis=-1)
                return (
                    grad_query,
                    lax.dynamic_update_index_in_dim(buffer_now, updated, safe_slot, 0),
                )

            return (
                lax.cond(
                    tile_slots[step_index] >= 0,
                    backward_take_tile,
                    lambda inner_state: inner_state,
                    back_state,
                ),
                None,
            )

        start_state = (jnp.zeros((tile_rows, head_count, head_width), jnp.float32), key_buffer)
        (grad_query, key_buffer), _ = lax.scan(backward, start_state, step_order)
        attention_low = attention.reshape(tile_rows, query_width).astype(jnp.bfloat16)
        return (
            key_buffer,
            (attention_low, grad_query.reshape(tile_rows, query_width).astype(jnp.bfloat16)),
        )

    empty_buffer = jnp.zeros((pack_tiles.shape[0], tile_rows, 2 * head_width), jnp.float32)
    key_buffer, (attention_low, grad_queries) = lax.scan(
        tile_pass, empty_buffer, jnp.arange(tile_count, dtype=jnp.int32)
    )
    summed = lax.psum_scatter(
        key_buffer.astype(jnp.bfloat16), "seq", scatter_dimension=0, tiled=True
    ).astype(jnp.float32)
    grad_keys = summed[..., :head_width].astype(jnp.bfloat16)
    grad_values = summed[..., head_width:].astype(jnp.bfloat16)
    flat_attention = attention_low.reshape(tile_count * tile_rows, query_width)
    columns = flat_grads
    weight_total = lax.psum_scatter(
        lax.dot_general(
            columns, flat_attention, (((0,), (0,)), ((), ())), preferred_element_type=jnp.float32
        ),
        ("dp", "seq"),
        scatter_dimension=0,
        tiled=True,
    )
    token_count = lax.axis_size("dp") * lax.axis_size("seq") * tile_count * tile_rows
    grad_weight = weight_total / math.sqrt(token_count)
    return (grad_queries[None], grad_keys[None], grad_values[None], grad_weight)


def solution(mesh):
    placed = (
        P("dp", "seq", None, None),
        P("dp", "seq", None, None),
        P("dp", "seq", None, None),
        P("dp", "seq", None, None),
        P("dp", None),
        P("dp", None, None),
        P("dp", None),
        P("dp", None),
    )
    return jax.shard_map(
        per_device,
        mesh=mesh,
        in_specs=placed,
        out_specs=(
            P("dp", "seq", None, None),
            P("dp", "seq", None, None),
            P("dp", "seq", None, None),
            P(("dp", "seq"), None),
        ),
        check_vma=False,
    )
```

profile of v0, /device:TPU:4, one launch (start us, length us, event | category | flops | bytes accessed | tf_op | source)
XLA Modules:
  0.0 1695.7 jit_solution(5170402476819762064)
XLA Ops:
  7.2 1.7 pad_maximum_fusion
  15.9 96.8 %all-gather.3.cloned.1.call-done = bf16[32,512,256]{2,1,0:T(8,128)(2,1)} async-done(((bf16[1,512,256]{2,1,0:T(8,128)(2,1)}), bf16[32,512,256]{2,1,0:T(8,128)(2,1)}) %all-gather.3.cloned.1.call-update) | async-done | bytes 8388624 | tf_op jit(solution)/shard_map/all_gather | solution.py:42
  112.8 55.6 %while.41 = (s32[]{:T(128)}, f32[512,4]{0,1:T(4,128)S(1)}, f32[512,4]{0,1:T(4,128)S(1)}, f32[512,4,128]{2,0,1:T(8,128)S(1)}, s32[4]{0:T(128)S(1)}, /*index=5*/s3...) while((s32[]{:T(128)}, f32[512,4]{0,1:T(4,128)S(1)}, ...), condition=%wide.region_8.9_spmd, body=%wide.region_3.8_spmd.sunk | while | flops 551817728 | bytes 17171872 | solution.py:116
  116.6 10.1 conditional.4
  124.8 1.9 fusion.6
  130.5 10.1 conditional.4
  138.7 1.9 fusion.6
  144.4 10.1 conditional.4
  152.6 1.9 fusion.6
  158.3 10.1 conditional.4
  166.4 1.9 fusion.6
  168.8 6.1 fusion.42
  174.9 5.9 fusion.34
  181.1 7.9 broadcast_in_dim.134
  189.0 71.3 %while.42 = (s32[]{:T(128)}, f32[512,4,128]{2,0,1:T(8,128)S(1)}, f32[32,512,256]{1,2,0:T(8,128)}, s32[4]{0:T(128)S(1)}, s32[4]{0:T(128)S(1)}, /*index=5*/s32[32]...) while((s32[]{:T(128)}, f32[512,4,128]{2,0,1:T(8,128)S(1)}, ...), condition=%wide.region_13.14_spmd, body=%wide.region_10.13_spmd.sunk | while | flops 1357120000 | bytes 26896304 | solution.py:163
  192.8 14.1 conditional.5
  201.4 1.8 fusion.16
  204.9 1.9 fusion.29
  210.6 14.1 conditional.5
  217.6 1.6 fusion.24
  219.2 1.8 fusion.16
  222.7 1.9 fusion.29
  228.4 14.1 conditional.5
  237.0 1.8 fusion.16
  240.6 1.9 fusion.29
  246.3 14.0 conditional.5
  254.9 1.8 fusion.16
  258.4 1.9 fusion.29
  260.3 13.8 copy.60
  275.7 1029.0 %reduce-scatter.5.cloned.1.call-done = f32[16,512]{1,0:T(8,128)} async-done(((f32[4096,512]{1,0:T(8,128)}), f32[16,512]{1,0:T(8,128)}) %reduce-scatter.5.cloned.1.call-update) | async-done | bytes 32784 | tf_op jit(solution)/shard_map/reduce_scatter | solution.py:181
  1306.0 381.5 %reduce-scatter.3.cloned.1.call-done = bf16[1,512,256]{2,1,0:T(8,128)(2,1)} async-done(((bf16[32,512,256]{2,1,0:T(8,128)(2,1)}), bf16[1,512,256]{2,1,0:T(8,128)(2,1)}) %reduce-scatter.3.cloned.1.call-update) | async-done | bytes 262160 | tf_op jit(solution)/shard_map/reduce_scatter | solution.py:174
  1687.5 1.7 slice_bitcast_fusion.9
  (127 shorter events, 66.0 us)
Async XLA Ops:
  7.2 105.5 %all-gather.3.cloned.1.call-start = ((), (), s32[]{:S(2)}) async-start(), calls=%async_computation.2 | async-start | bytes 8650752 | tf_op jit(solution)/shard_map/all_gather | solution.py:42
  8.9 159.8 %all-gather.5.cloned.1.call-start = ((), (), s32[]{:S(2)}) async-start(), calls=%async_computation.3 | async-start | bytes 4718592 | tf_op jit(solution)/shard_map/all_gather | solution.py:51
  9.7 1295.0 %reduce-scatter.5.cloned.1.call-start = ((), (), s32[]{:S(2)}) async-start(), calls=%async_computation.5 | async-start | bytes 8421376 | tf_op jit(solution)/shard_map/reduce_scatter | solution.py:181
  168.8 6.1 copy-start
  180.8 1506.7 %reduce-scatter.3.cloned.1.call-start = ((), (), s32[]{:S(2)}) async-start(), calls=%async_computation.4 | async-start | bytes 8650752 | tf_op jit(solution)/shard_map/reduce_scatter | solution.py:174
Sparse Core Ops, SparseCore 0:
  11.2 101.5 all-gather.2
  114.6 30.4 all-gather.4
  180.9 1123.6 reduce-scatter.4
  1309.0 378.4 reduce-scatter.2
where the time goes:
time: 1700 us
  waiting for transfers between devices  1510 us (89%)
  local copies, waits for them, and re-layouts  55.1 us (3%)
  loops' own time  47.3 us (3%)
  matrix products  46.1 us (3%)
  other arithmetic  24.8 us (1%)
    reduce_scatter x1, waiting for transfers between devices, per_device(): lax.psum_scatter(lax.dot_general(columns, flat_attention, (((0,), (0,)),...  1030 us
    reduce_scatter x1, waiting for transfers between devices, per_device(): lax.psum_scatter(key_buffer.astype(jnp.bfloat16), 'seq', scatter_dimensio...  381 us
    all_gather x1, waiting for transfers between devices, per_device(): pack_tiles = lax.all_gather(key_values, 'seq', axis=0, tiled=True)  96.8 us
  transfers between devices with their start and end apart: 4, of which 3 were waited for; matrix products, arithmetic and copies ran while one was open for 7% of the time, Pallas kernels for 0%

commit v1 on v0

v1 whole, which is shorter than its diff:
```python
import math

import jax
import jax.numpy as jnp
from jax import lax
from jax.experimental import pallas as pl
from jax.experimental.pallas import tpu as pltpu
from jax.sharding import Mesh, PartitionSpec as P

BF = jnp.bfloat16
F32 = jnp.float32
MASKED = -1e30
LOG2E = 1.0 / math.log(2.0)
VMEM_LIMIT = 48 * 1024 * 1024
SMEM_SPEC = pl.BlockSpec(memory_space=pltpu.SMEM)
VMEM_SPEC = pl.BlockSpec(memory_space=pltpu.VMEM)
ROWS = 256


def nn(a, b):
    return lax.dot_general(a, b, (((1,), (0,)), ((), ())), preferred_element_type=F32)


def tn(a, b):
    return lax.dot_general(a, b, (((0,), (0,)), ((), ())), preferred_element_type=F32)


def params():
    return pltpu.CompilerParams(vmem_limit_bytes=VMEM_LIMIT)


def route_kernel(me_ref, anc_ref, owner_ref, len_ref, chunk_ref, out_ref, info_ref):
    nodes, depth = anc_ref.shape
    me = me_ref[0]

    def one_node(n, carry):
        slot = owner_ref[n]
        mine = slot == me

        @pl.when(mine)
        def _():
            info_ref[depth] = len_ref[n]

        for k in range(depth):
            a = anc_ref[n, k]
            present = a >= 0
            safe = jnp.maximum(a, 0)
            source = owner_ref[safe]

            @pl.when(present)
            def _():
                out_ref[slot, k] = chunk_ref[source]

            @pl.when(jnp.logical_not(present))
            def _():
                out_ref[slot, k] = jnp.zeros(out_ref.shape[2:], out_ref.dtype)

            @pl.when(mine)
            def _():
                info_ref[k] = jnp.where(present, len_ref[safe], 0)

        return carry

    lax.fori_loop(0, nodes, one_node, 0)


def route(me, anc, owner, lengths, chunks):
    nodes, depth = anc.shape
    return pl.pallas_call(
        route_kernel,
        out_shape=(
            jax.ShapeDtypeStruct((nodes, depth) + chunks.shape[1:], BF),
            jax.ShapeDtypeStruct((depth + 1,), jnp.int32),
        ),
        in_specs=[SMEM_SPEC] * 4 + [VMEM_SPEC],
        out_specs=(VMEM_SPEC, SMEM_SPEC),
        compiler_params=params(),
        name="route",
    )(me, anc, owner, lengths, chunks)


def load_tiles(self_ref, anc_ref, kt_ref, vt_ref, k_ref=None, v_ref=None):
    head = kt_ref.shape[0]
    tile = self_ref.shape[0]
    depth = anc_ref.shape[1]
    for j in range(depth + 1):
        if j < depth:
            kv = anc_ref[:, j].reshape(tile, 2 * head)
        else:
            kv = self_ref[...]
        k_part, v_part = kv[:, :head], kv[:, head:]
        at = slice(j * tile, (j + 1) * tile)
        kt_ref[:, at] = k_part.T
        if vt_ref is not None:
            vt_ref[:, at] = v_part.T
        if k_ref is not None:
            k_ref[at] = k_part
        if v_ref is not None:
            v_ref[at] = v_part


def fill_bias(info_ref, bias_ref, tile):
    tiles = bias_ref.shape[1] // tile
    pos = lax.broadcasted_iota(jnp.int32, (1, tile), 1)
    for j in range(tiles):
        bias_ref[:, j * tile : (j + 1) * tile] = jnp.where(pos < info_ref[j], 0.0, MASKED)


def block_logits(q, kt_ref, bias_ref, first, width, tile, scale):
    s = nn(q, kt_ref[:, :width]) * scale + bias_ref[:, :width]
    base = kt_ref.shape[1] - tile + first
    q_pos = lax.broadcasted_iota(jnp.int32, (ROWS, ROWS), 0)
    k_pos = lax.broadcasted_iota(jnp.int32, (ROWS, ROWS), 1)
    diagonal = jnp.where(k_pos <= q_pos, s[:, base : base + ROWS], MASKED)
    return jnp.concatenate([s[:, :base], diagonal], axis=1)


def forward_kernel(info_ref, q_ref, g_ref, self_ref, anc_ref, att_ref, stat_ref, kt_ref, v_ref, bias_ref):
    tile, width = q_ref.shape
    head = kt_ref.shape[0]
    heads = width // head
    depth = anc_ref.shape[1]
    length = info_ref[depth]
    load_tiles(self_ref, anc_ref, kt_ref, None, None, v_ref)
    fill_bias(info_ref, bias_ref, tile)
    scale = LOG2E / math.sqrt(head)
    for first in range(0, tile, ROWS):
        at = slice(first, first + ROWS)
        keys = depth * tile + first + ROWS
        row_ok = first + lax.broadcasted_iota(jnp.int32, (ROWS, 1), 0) < length
        for h in range(heads):
            cols = slice(h * head, (h + 1) * head)
            s = block_logits(q_ref[at, cols], kt_ref, bias_ref, first, keys, tile, scale)
            top = jnp.max(s, axis=1, keepdims=True)
            w = jnp.exp2(s - top)
            total = jnp.sum(w, axis=1, keepdims=True)
            att = nn(w.astype(BF), v_ref[:keys]) / total
            g = jnp.where(row_ok, g_ref[at, cols], jnp.zeros((), BF)).astype(F32)
            stat_ref[at, h : h + 1] = top + jnp.log2(total)
            stat_ref[at, heads + h : heads + h + 1] = jnp.sum(g * att, axis=1, keepdims=True)
            att_ref[at, cols] = jnp.where(row_ok, att, 0.0).astype(BF)


def forward(info, q, g, kv_self, kv_anc):
    tile, width = q.shape
    head = kv_self.shape[1] // 2
    keys = (kv_anc.shape[1] + 1) * tile
    return pl.pallas_call(
        forward_kernel,
        out_shape=(
            jax.ShapeDtypeStruct((tile, width), BF),
            jax.ShapeDtypeStruct((tile, 2 * (width // head)), F32),
        ),
        in_specs=[SMEM_SPEC] + [VMEM_SPEC] * 4,
        out_specs=(VMEM_SPEC, VMEM_SPEC),
        scratch_shapes=[
            pltpu.VMEM((head, keys), BF),
            pltpu.VMEM((keys, head), BF),
            pltpu.VMEM((1, keys), F32),
        ],
        compiler_params=params(),
        name="forward",
    )(info, q, g, kv_self, kv_anc)


def backward_kernel(
    info_ref, q_ref, g_ref, stat_ref, self_ref, anc_ref,
    dq_ref, term_ref, own_ref,
    kt_ref, vt_ref, k_ref, bias_ref, dk_ref, dv_ref,
):
    tile, width = q_ref.shape
    head = kt_ref.shape[0]
    heads = width // head
    depth = anc_ref.shape[1]
    length = info_ref[depth]
    load_tiles(self_ref, anc_ref, kt_ref, vt_ref, k_ref)
    fill_bias(info_ref, bias_ref, tile)
    root = 1.0 / math.sqrt(head)
    scale = LOG2E * root
    dk_ref[...] = jnp.zeros_like(dk_ref)
    dv_ref[...] = jnp.zeros_like(dv_ref)
    for first in range(0, tile, ROWS):
        at = slice(first, first + ROWS)
        keys = depth * tile + first + ROWS
        row_ok = first + lax.broadcasted_iota(jnp.int32, (ROWS, 1), 0) < length
        for h in range(heads):
            cols = slice(h * head, (h + 1) * head)
            q = q_ref[at, cols]
            g = jnp.where(row_ok, g_ref[at, cols], jnp.zeros((), BF))
            s = block_logits(q, kt_ref, bias_ref, first, keys, tile, scale)
            p = jnp.exp2(s - stat_ref[at, h : h + 1])
            dp = nn(g, vt_ref[:, :keys])
            ds = (p * (dp - stat_ref[at, heads + h : heads + h + 1])).astype(BF)
            p = p.astype(BF)
            dq_ref[at, cols] = (nn(ds, k_ref[:keys]) * root).astype(BF)
            dk_ref[:keys] += tn(ds, q)
            dv_ref[:keys] += tn(p, g)
    for j in range(depth):
        rows = slice(j * tile, (j + 1) * tile)
        shape = (tile // 16, 16, head)
        term_ref[:, j, :, :head] = (dk_ref[rows] * root).astype(BF).reshape(shape)
        term_ref[:, j, :, head:] = dv_ref[rows].astype(BF).reshape(shape)
    own_ref[:, :head] = dk_ref[depth * tile :] * root
    own_ref[:, head:] = dv_ref[depth * tile :]


def backward(info, q, g, stat, kv_self, kv_anc):
    tile, width = q.shape
    head = kv_self.shape[1] // 2
    keys = (kv_anc.shape[1] + 1) * tile
    return pl.pallas_call(
        backward_kernel,
        out_shape=(
            jax.ShapeDtypeStruct((tile, width), BF),
            jax.ShapeDtypeStruct(kv_anc.shape, BF),
            jax.ShapeDtypeStruct((tile, 2 * head), F32),
        ),
        in_specs=[SMEM_SPEC] + [VMEM_SPEC] * 5,
        out_specs=(VMEM_SPEC,) * 3,
        scratch_shapes=[
            pltpu.VMEM((head, keys), BF),
            pltpu.VMEM((head, keys), BF),
            pltpu.VMEM((keys, head), BF),
            pltpu.VMEM((1, keys), F32),
            pltpu.VMEM((keys, head), F32),
            pltpu.VMEM((keys, head), F32),
        ],
        compiler_params=params(),
        name="backward",
    )(info, q, g, stat, kv_self, kv_anc)


def collect_kernel(anc_ref, owner_ref, term_ref, *refs):
    part_refs, (out_ref, sum_ref) = refs[:-2], refs[-2:]
    nodes, depth = anc_ref.shape
    width = term_ref.shape[3]
    sum_ref[...] = jnp.zeros_like(sum_ref)

    def one_node(n, carry):
        slot = owner_ref[n]
        for k in range(depth):
            a = anc_ref[n, k]

            @pl.when(a >= 0)
            def _():
                target = owner_ref[jnp.maximum(a, 0)]
                sum_ref[target] += term_ref[slot, k].astype(F32)

        return carry

    lax.fori_loop(0, nodes, one_node, 0)
    out_ref[:, :, :width] = sum_ref[...].astype(BF)
    total = part_refs[0][...].astype(F32)
    for part in part_refs[1:]:
        total = total + part[...].astype(F32)
    out_ref[:, :, width:] = total.astype(BF).reshape(out_ref.shape[0], 16, -1)


def collect(anc, owner, terms, parts):
    nodes = anc.shape[0]
    width = terms.shape[3]
    return pl.pallas_call(
        collect_kernel,
        out_shape=jax.ShapeDtypeStruct((nodes, 16, width + parts[0].shape[1]), BF),
        in_specs=[SMEM_SPEC] * 2 + [VMEM_SPEC] * (1 + len(parts)),
        out_specs=VMEM_SPEC,
        scratch_shapes=[pltpu.VMEM((nodes, 16, width), F32)],
        compiler_params=params(),
        name="collect",
    )(anc, owner, terms, *parts)


def finish_kernel(weight_scale, got_ref, own_ref, gk_ref, gv_ref, gw_ref):
    tile, width = own_ref.shape
    head = width // 2
    total = got_ref[:, :, :width].reshape(tile, width).astype(F32) + own_ref[...]
    gk_ref[...] = total[:, :head].astype(BF)
    gv_ref[...] = total[:, head:].astype(BF)
    gw_ref[...] = jnp.sum(got_ref[:, :, width:].astype(F32), axis=0) * weight_scale


def finish(got, own, weight_scale):
    tile, width = own.shape
    return pl.pallas_call(
        lambda *refs: finish_kernel(weight_scale, *refs),
        out_shape=(
            jax.ShapeDtypeStruct((tile, width // 2), BF),
            jax.ShapeDtypeStruct((tile, width // 2), BF),
            jax.ShapeDtypeStruct((16, got.shape[2] - width), F32),
        ),
        in_specs=[VMEM_SPEC] * 2,
        out_specs=(VMEM_SPEC,) * 3,
        compiler_params=params(),
        name="finish",
    )(got, own)


def ring(size, step):
    return [(i, (i + step) % size) for i in range(size)]


def per_device(queries, keys, values, grad_out, out_weight, ancestors, owner, lengths):
    q = queries[0, 0]
    tile, width = q.shape
    head = keys.shape[-1]
    seq = ("z", "y")
    nodes = lax.axis_size(seq)
    xs = lax.axis_size("x")
    core = lax.axis_index("core")
    x = lax.axis_index("x")
    me = lax.axis_index(seq).astype(jnp.int32).reshape(1)
    anc, own_row, len_row = ancestors[0], owner[0], lengths[0]

    weight = lax.all_gather(out_weight, ("x", "core"), axis=0, tiled=True)
    grads = grad_out[0, 0]
    block = grads.shape[1] // (2 * xs)
    halves = grads.reshape(tile, xs, 2, block)
    mine = lax.dynamic_index_in_dim(halves, core, 2, keepdims=False).reshape(tile, xs * block)
    other = lax.dynamic_index_in_dim(halves, 1 - core, 2, keepdims=False).reshape(tile, xs * block)
    sibling = lax.ppermute(other, "core", ring(2, 1))

    kv_self = jnp.concatenate([keys[0, 0], values[0, 0]], axis=-1)
    chunks = lax.all_to_all(kv_self.reshape(nodes, 16, 2 * head), seq, 0, 0, tiled=True)
    routed, info = route(me, anc, own_row, len_row, chunks)
    kv_anc = lax.all_to_all(routed, seq, 0, 0, tiled=True)

    grad_att = jnp.dot(grads, weight, preferred_element_type=F32).astype(BF)
    att, stat = forward(info, q, grad_att, kv_self, kv_anc)

    att_sibling = lax.ppermute(att, "core", ring(2, 1))
    both_grads = jnp.concatenate([mine, sibling], axis=0)
    both_att = jnp.concatenate([att, att_sibling], axis=0)
    product = tn(both_grads, both_att).astype(BF).reshape(xs, block, width)
    parts = [lax.dynamic_index_in_dim(product, x, 0, keepdims=False)]
    for step in range(1, xs):
        piece = lax.dynamic_index_in_dim(product, (x + step) % xs, 0, keepdims=False)
        parts.append(lax.ppermute(piece, "x", ring(xs, step)))

    grad_q, terms, own = backward(info, q, grad_att, stat, kv_self, kv_anc)
    terms = lax.all_to_all(terms, seq, 0, 0, tiled=True)
    summed = collect(anc, own_row, terms, parts)
    got = lax.all_to_all(summed, seq, 0, 0, tiled=True)
    token_count = 2 * xs * nodes * tile
    grad_k, grad_v, grad_w = finish(got, own, 1.0 / math.sqrt(token_count))
    return grad_q[None, None], grad_k[None, None], grad_v[None, None], grad_w


def solution(mesh):
    dp, seq = mesh.devices.shape
    fine = Mesh(mesh.devices.reshape(dp // 2, 2, seq // 4, 4), ("x", "core", "z", "y"))
    d, s = ("x", "core"), ("z", "y")
    placed = (
        P(d, s, None, None),
        P(d, s, None, None),
        P(d, s, None, None),
        P(d, s, None, None),
        P(d, None),
        P(d, None, None),
        P(d, None),
        P(d, None),
    )
    return jax.shard_map(
        per_device,
        mesh=fine,
        in_specs=placed,
        out_specs=(
            P(d, s, None, None),
            P(d, s, None, None),
            P(d, s, None, None),
            P(d + s, None),
        ),
        check_vma=False,
    )
```

time: 1700 us -> 174 us (0.10)
  waiting for transfers between devices: 1510 us -> 43.4 us
  loops' own time: 47.3 us -> 0 us
  local copies, waits for them, and re-layouts: 55.1 us -> 13.3 us
  matrix products: 46.1 us -> 10.4 us
  blocking collectives: 0 us -> 31.1 us
  Pallas kernels: 0 us -> 28.9 us
  starting transfers between devices: 0.34 us -> 28.6 us
  other arithmetic: 24.8 us -> 1.73 us
    reduce_scatter x2 -> x0, waiting for transfers between devices: 1410 us -> none  [the longest x1 1030 us: per_device(): lax.psum_scatter(lax.dot_general(columns, flat_attention, (((0,), (0,)),...]
    all_gather x2 -> x1, waiting for transfers between devices: 96.8 us -> 0.5 us  [per_device(): weight = lax.all_gather(out_weight, ('x', 'core'), axis=0, tiled=True)]
    another operation x10 -> x0, loops' own time: 47.3 us -> none  [the longest x4 13.2 us: forward(): lax.cond(tile_slots[step_index] >= 0, forward_take_tile, lambda forward_s...]
    dot_general x30 -> x2, matrix products: 46.1 us -> 10.4 us  [the longest x1 5.79 us: per_device(): grad_att = jnp.dot(grads, weight, preferred_element_type=F32).astype(BF)]
    all_to_all x0 -> x1, blocking collectives: none -> 31.1 us  [per_device(): got = lax.all_to_all(summed, seq, 0, 0, tiled=True)]
    pallas_call x0 -> x5, Pallas kernels: none -> 28.9 us  [the longest x1 13.7 us: backward(): pl.pallas_call(backward_kernel, out_shape=(jax.ShapeDtypeStruct((tile, wi...]
    all_to_all x0 -> x3, starting transfers between devices: none -> 25.4 us  [the longest x1 11.5 us: per_device(): lax.all_to_all(kv_self.reshape(nodes, 16, 2 * head), seq, 0, 0, tiled=True)]
    ppermute x0 -> x5, waiting for transfers between devices: none -> 24 us  [the longest x3 24 us: per_device(): parts.append(lax.ppermute(piece, 'x', ring(xs, step)))]
  transfers between devices with their start and end apart: 4 -> 9, of which waited for: 3 -> 6; matrix products, arithmetic and copies ran while one was open for 7% -> 14% of each run, Pallas kernels for 0% -> 15%
where the time goes in v1:
time: 174 us; the launch traced here: 172 us
  waiting for transfers between devices  43.4 us (25%)
  blocking collectives  31.1 us (18%)
  Pallas kernels  28.9 us (17%)
  starting transfers between devices  28.6 us (16%)
  between operations  14.2 us (8%)
  local copies, waits for them, and re-layouts  13.3 us (8%)
  matrix products  10.4 us (6%)
    all_to_all x1, blocking collectives, per_device(): got = lax.all_to_all(summed, seq, 0, 0, tiled=True)  31.1 us
    ppermute x3, waiting for transfers between devices, per_device(): parts.append(lax.ppermute(piece, 'x', ring(xs, step)))  24 us
    all_to_all x1, waiting for transfers between devices, per_device(): kv_anc = lax.all_to_all(routed, seq, 0, 0, tiled=True)  16.8 us
    pallas_call x1, Pallas kernels, backward(): pl.pallas_call(backward_kernel, out_shape=(jax.ShapeDtypeStruct((tile, wi...  13.7 us
    all_to_all x1, starting transfers between devices, per_device(): lax.all_to_all(kv_self.reshape(nodes, 16, 2 * head), seq, 0, 0, tiled=True)  11.5 us
    unnamed x17, local copies, waits for them, and re-layouts  8.45 us
    all_to_all x1, starting transfers between devices, per_device(): kv_anc = lax.all_to_all(routed, seq, 0, 0, tiled=True)  8.42 us
    pallas_call x1, Pallas kernels, forward(): pl.pallas_call(forward_kernel, out_shape=(jax.ShapeDtypeStruct((tile, wid...  8.4 us
  transfers between devices with their start and end apart: 9, of which 6 were waited for; matrix products, arithmetic and copies ran while one was open for 14% of the time, Pallas kernels for 15%

profile of v1, /device:TPU:4, one launch (start us, length us, event | category | flops | bytes accessed | tf_op | source)
XLA Modules:
  0.0 171.7 jit_solution(6386380295620082186)
XLA Ops:
  7.2 0.0 all-gather.2.cloned.1.call-start
  7.2 0.7 all-gather.2.cloned.1.call-update
  7.9 1.7 pad_maximum_fusion
  9.6 11.5 %all-to-all-start = ((bf16[32,16,256]{2,1,0:T(8,128)(2,1)}), bf16[32,16,256]{2,1,0:T(8,128)(2,1)S(1)}, u32[]{:S(2)}, u32[]{:S(2)}) async-start(bf16[32,16,256]{2,1,0:T(8,128)(2,1)} %pad_maximum_fusion), calls=%async_computation | async-start | bytes 524288 | tf_op jit(solution)/shard_map/all_to_all | solution.py:323
  21.1 6.6 %copy.17 = bf16[1,1,512,4096]{2,3,1,0:T(8,128)(2,1)} copy(bf16[1,1,512,4096]{3,2,1,0:T(8,128)(2,1)} %param.11) | data formatting | bytes 8388608 | tf_op args[3]
  27.7 0.0 copy-start.6
  27.7 4.6 %constant_dynamic-slice_fusion.1 = (bf16[512,4,1,512]{0,3,2,1:T(8,128)(2,1)}, bf16[512,4,1,512]{0,3,2,1:T(8,128)(2,1)}) fusion(bf16[512,4,2,512]{0,3,2,1:T(8,128)(2,1)} %bitcast.37, s32[]{:T(128)S(6)} %select_n.35, s32[]{:T(128)S(6)} %select_n.36), kind=kLoop, calls=%fused_computation.18 | loop fusion | bytes 8388616 | tf_op jit(solution)/shard_map/jit(dynamic_index_in_dim)/dynamic_slice | solution.py:318
  32.3 0.1 copy.19
  32.4 1.3 all-to-all-done.chunk_ref
  33.8 3.4 %route.1 = (bf16[32,3,16,256]{3,2,1,0:T(8,128)(2,1)}, s32[4]{0:T(128)S(1)}) custom-call(s32[1]{0:T(128)} %bitcast.me_ref, s32[32,3]{1,0:T(8,128)S(1)} %bitcast.32, s32[32]{0:T(128)S(1)} %bitcast.34, s32[32]{0:T(128)S(1)} %bitcast.36, bf16[32,16,256]{2,1,0:T(8,128)(2,1)S(1)} %all-to-all-done.chunk_ref), custom_call_target="tpu_custom_call" | custom-call | tf_op jit(solution)/shard_map/route/pallas_call | solution.py:69
  37.2 8.4 %all-to-all-start.1 = ((bf16[32,3,16,256]{3,2,1,0:T(8,128)(2,1)}), bf16[32,3,16,256]{3,2,1,0:T(8,128)(2,1)S(1)}, u32[]{:S(2)}, u32[]{:S(2)}) async-start(bf16[32,3,16,256]{3,2,1,0:T(8,128)(2,1)} %get-tuple-element.15), calls=%async_computation.1 | async-start | bytes 1572864 | tf_op jit(solution)/shard_map/all_to_all | solution.py:325
  45.7 0.0 copy-start
  45.7 0.5 all-gather.2.cloned.1.call-done
  46.2 5.8 %fusion.9.g_ref = bf16[512,512]{1,0:T(8,128)(2,1)S(1)} fusion(bf16[4096,512]{1,0:T(8,128)(2,1)} %all-gather.2.cloned.1.call-done, bf16[1,1,512,4096]{3,2,1,0:T(8,128)(2,1)} %param.11), kind=kOutput, calls=%fused_computation.7 | convolution fusion | flops 2147745792 | bytes 8912896 | tf_op jit(solution)/shard_map/dot_general | solution.py:327
  52.0 16.8 %all-to-all-done.1.anc_ref = bf16[32,3,16,256]{3,2,1,0:T(8,128)(2,1)S(1)} async-done(((bf16[32,3,16,256]{3,2,1,0:T(8,128)(2,1)}), bf16[32,3,16,256]{3,2,1,0:T(8,128)(2,1)S(1)}, u32[]{:S(2)}, u32[]{:S(2)}) %all-to-all-start.1) | async-done | bytes 786464 | tf_op jit(solution)/shard_map/all_to_all | solution.py:325
  68.8 8.4 %forward.1 = (bf16[512,512]{1,0:T(8,128)(2,1)}, f32[512,8]{1,0:T(8,128)S(1)}) custom-call(s32[4]{0:T(128)S(1)} %get-tuple-element.14.info_ref, bf16[512,512]{1,0:T(8,128)(2,1)S(1)} %bitcast.30, bf16[512,512]{1,0:T(8,128)(2,1)S(1)} %fusion.9.g_ref, bf16[512,256]{1,0:T(8,128)(2,1)S(1)} %pad_maximum_fusion.1.self_ref, ...), custom_call_target="tpu_custom_call" | custom-call | tf_op jit(solution)/shard_map/forward/pallas_call | solution.py:148
  77.2 0.0 collective-permute-start.1
  77.2 13.7 %backward.1 = (bf16[512,512]{1,0:T(8,128)(2,1)}, bf16[32,3,16,256]{3,2,1,0:T(8,128)(2,1)}, f32[512,256]{1,0:T(8,128)S(1)}) custom-call(s32[4]{0:T(128)S(1)} %get-tuple-element.14.info_ref, bf16[512,512]{1,0:T(8,128)(2,1)S(1)} %bitcast.31, bf16[512,512]{1,0:T(8,128)(2,1)S(1)} %fusion.9.g_ref, f32[512,8]{1,0:T(8,128)S(1)} %get-tuple-element.16.stat_ref, ...), custom_call_target="tpu_custom_call" | custom-call | tf_op jit(solution)/shard_map/backward/pallas_call | solution.py:211
  90.9 5.5 %all-to-all-start.2 = ((bf16[32,3,16,256]{3,2,1,0:T(8,128)(2,1)}), bf16[32,3,16,256]{3,2,1,0:T(8,128)(2,1)S(1)}, u32[]{:S(2)}, u32[]{:S(2)}) async-start(bf16[32,3,16,256]{3,2,1,0:T(8,128)(2,1)} %get-tuple-element.18), calls=%async_computation.2 | async-start | bytes 1572864 | tf_op jit(solution)/shard_map/all_to_all | solution.py:340
  96.4 4.6 %fusion.6 = bf16[2048,512]{1,0:T(8,128)(2,1)S(1)} fusion(bf16[512,2048]{0,1:T(8,128)(2,1)} %collective-permute-done, bf16[512,2048]{0,1:T(8,128)(2,1)} %bitcast.38, bf16[512,512]{1,0:T(8,128)(2,1)S(1)} %collective-permute-done.1, bf16[512,512]{1,0:T(8,128)(2,1)} %get-tuple-element.19), kind=kOutput, calls=%fused_computation.6 | convolution fusion | flops 2159017984 | bytes 7340032 | tf_op jit(solution)/shard_map/dot_general | solution.py:25
  101.1 0.2 dynamic-slice_bitcast_fusion
  101.3 1.2 collective-permute-start.2
  102.5 0.8 collective-permute-start.3
  103.3 1.1 collective-permute-start.4
  104.5 11.7 %collective-permute-done.2.refs_1_ = bf16[512,512]{1,0:T(8,128)(2,1)S(1)} collective-permute-done((bf16[512,512]{1,0:T(8,128)(2,1)S(1)}, bf16[512,512]{1,0:T(8,128)(2,1)S(1)}, u32[]{:S(2)}, u32[]{:S(2)}) %collective-permute-start.2) | collective-permute-done | bytes 524320 | tf_op jit(solution)/shard_map/ppermute | solution.py:337
  116.1 10.5 %collective-permute-done.3.refs_2_ = bf16[512,512]{1,0:T(8,128)(2,1)S(1)} collective-permute-done((bf16[512,512]{1,0:T(8,128)(2,1)S(1)}, bf16[512,512]{1,0:T(8,128)(2,1)S(1)}, u32[]{:S(2)}, u32[]{:S(2)}) %collective-permute-start.3) | collective-permute-done | bytes 524320 | tf_op jit(solution)/shard_map/ppermute | solution.py:337
  126.6 1.8 %collective-permute-done.4.refs_3_ = bf16[512,512]{1,0:T(8,128)(2,1)S(1)} collective-permute-done((bf16[512,512]{1,0:T(8,128)(2,1)S(1)}, bf16[512,512]{1,0:T(8,128)(2,1)S(1)}, u32[]{:S(2)}, u32[]{:S(2)}) %collective-permute-start.4) | collective-permute-done | bytes 524320 | tf_op jit(solution)/shard_map/ppermute | solution.py:337
  128.5 0.8 copy-done.1
  129.3 1.0 copy-done.2
  130.3 2.6 %collect.1 = bf16[32,16,768]{2,1,0:T(8,128)(2,1)S(1)} custom-call(s32[32,3]{1,0:T(8,128)S(1)} %bitcast.33, s32[32]{0:T(128)S(1)} %bitcast.35, bf16[32,3,16,256]{3,2,1,0:T(8,128)(2,1)S(1)} %all-to-all-done.2.term_ref, bf16[512,512]{1,0:T(8,128)(2,1)S(1)} %get-tuple-element.29.refs_0_, bf16[512,512]{1,0:T(8,128)(2,1)S(1)} %collective-permute-done.2.refs_1_, ...), custom_call_target="tpu_custom_call" | custom-call | tf_op jit(solution)/shard_map/collect/pallas_call | solution.py:262
  133.0 31.1 %all_to_all.20.refs_0_ = bf16[32,16,768]{2,1,0:T(8,128)(2,1)S(1)} all-to-all(bf16[32,16,768]{2,1,0:T(8,128)(2,1)S(1)} %collect.1), channel_id=1, replica_groups=mesh['x'=4,'core'=2,'z'=8,'y'=4] {'z','y'}, dimensions={0} | all-to-all | bytes 1572864 | tf_op jit(solution)/shard_map/all_to_all | solution.py:342
  164.1 0.8 finish.1
  (17 shorter events, 0.1 us)
Async XLA Ops:
  7.2 39.0 %all-gather.2.cloned.1.call-start = ((), (), s32[]{:S(2)}) async-start(), calls=%async_computation.4 | async-start | bytes 4718592 | tf_op jit(solution)/shard_map/all_gather | solution.py:314
  9.6 24.2 %all-to-all-start = ((bf16[32,16,256]{2,1,0:T(8,128)(2,1)}), bf16[32,16,256]{2,1,0:T(8,128)(2,1)S(1)}, u32[]{:S(2)}, u32[]{:S(2)}) async-start(bf16[32,16,256]{2,1,0:T(8,128)(2,1)} %pad_maximum_fusion), calls=%async_computation | async-start | bytes 524288 | tf_op jit(solution)/shard_map/all_to_all | solution.py:323
  27.7 4.7 %copy-start.7 = (s32[1,32,3]{1,0,2:T(1,128)S(1)}, s32[1,32,3]{1,0,2:T(1,128)}, u32[]{:S(2)}) copy-start(s32[1,32,3]{1,0,2:T(1,128)} %param.13) | copy-start | bytes 1156
  27.7 6.1 %copy-start.3 = (s32[1,32]{1,0:T(1,128)S(1)}, s32[1,32]{1,0:T(1,128)}, u32[]{:S(2)}) copy-start(s32[1,32]{1,0:T(1,128)} %param.14) | copy-start | bytes 388
  27.7 6.1 %copy-start.4 = (s32[1,32]{1,0:T(1,128)S(1)}, s32[1,32]{1,0:T(1,128)}, u32[]{:S(2)}) copy-start(s32[1,32]{1,0:T(1,128)} %param.15) | copy-start | bytes 388
  27.7 17.9 %copy-start.5 = (bf16[1,1,512,128]{3,2,1,0:T(8,128)(2,1)S(1)}, bf16[1,1,512,128]{3,2,1,0:T(8,128)(2,1)}, u32[]{:S(2)}) copy-start(bf16[1,1,512,128]{3,2,1,0:T(8,128)(2,1)} %param.10) | copy-start | bytes 393220
  27.7 17.9 %copy-start.6 = (bf16[1,1,512,128]{3,2,1,0:T(8,128)(2,1)S(1)}, bf16[1,1,512,128]{3,2,1,0:T(8,128)(2,1)}, u32[]{:S(2)}) copy-start(bf16[1,1,512,128]{3,2,1,0:T(8,128)(2,1)} %param.9) | copy-start | bytes 393220
  32.3 64.1 %collective-permute-start = (bf16[512,2048]{0,1:T(8,128)(2,1)}, bf16[512,2048]{0,1:T(8,128)(2,1)}, u32[]{:S(2)}, u32[]{:S(2)}) collective-permute-start(bf16[512,2048]{0,1:T(8,128)(2,1)} %bitcast.12), channel_id=1, source_target_pairs={{0,32},{32,0},{1,33},{33,1},{2,34},{34,2},{3,35},{35,3},{4,36},{36... | collective-permute-start | bytes 6291464 | tf_op jit(solution)/shard_map/ppermute | solution.py:320
  37.2 31.6 %all-to-all-start.1 = ((bf16[32,3,16,256]{3,2,1,0:T(8,128)(2,1)}), bf16[32,3,16,256]{3,2,1,0:T(8,128)(2,1)S(1)}, u32[]{:S(2)}, u32[]{:S(2)}) async-start(bf16[32,3,16,256]{3,2,1,0:T(8,128)(2,1)} %get-tuple-element.15), calls=%async_computation.1 | async-start | bytes 1572864 | tf_op jit(solution)/shard_map/all_to_all | solution.py:325
  45.7 23.1 %copy-start = (bf16[1,1,512,512]{3,2,1,0:T(8,128)(2,1)S(1)}, bf16[1,1,512,512]{3,2,1,0:T(8,128)(2,1)}, u32[]{:S(2)}) copy-start(bf16[1,1,512,512]{3,2,1,0:T(8,128)(2,1)} %param.8) | copy-start | bytes 1572868
  77.2 19.3 %collective-permute-start.1 = (bf16[512,512]{1,0:T(8,128)(2,1)}, bf16[512,512]{1,0:T(8,128)(2,1)S(1)}, u32[]{:S(2)}, u32[]{:S(2)}) collective-permute-start(bf16[512,512]{1,0:T(8,128)(2,1)} %get-tuple-element.19), channel_id=1, source_target_pairs={{0,32},{32,0},{1,33},{33,1},{2,34},{34,2},{3,35},{35,3},{4,36},{36... | collective-permute-start | bytes 1572872 | tf_op jit(solution)/shard_map/ppermute | solution.py:330
  90.9 38.4 %all-to-all-start.2 = ((bf16[32,3,16,256]{3,2,1,0:T(8,128)(2,1)}), bf16[32,3,16,256]{3,2,1,0:T(8,128)(2,1)S(1)}, u32[]{:S(2)}, u32[]{:S(2)}) async-start(bf16[32,3,16,256]{3,2,1,0:T(8,128)(2,1)} %get-tuple-element.18), calls=%async_computation.2 | async-start | bytes 1572864 | tf_op jit(solution)/shard_map/all_to_all | solution.py:340
  101.3 14.8 %collective-permute-start.2 = (bf16[512,512]{1,0:T(8,128)(2,1)S(1)}, bf16[512,512]{1,0:T(8,128)(2,1)S(1)}, u32[]{:S(2)}, u32[]{:S(2)}) collective-permute-start(bf16[512,512]{1,0:T(8,128)(2,1)S(1)} %get-tuple-element.28), channel_id=1, source_target_pairs={{0,64},{64,128},{128,192},{192,0},{1,65},{65,129},{129,193},{193,1... | collective-permute-start | bytes 1572872 | tf_op jit(solution)/shard_map/ppermute | solution.py:337
  102.5 24.1 %collective-permute-start.3 = (bf16[512,512]{1,0:T(8,128)(2,1)S(1)}, bf16[512,512]{1,0:T(8,128)(2,1)S(1)}, u32[]{:S(2)}, u32[]{:S(2)}) collective-permute-start(bf16[512,512]{1,0:T(8,128)(2,1)S(1)} %get-tuple-element.27), channel_id=1, source_target_pairs={{0,128},{64,192},{128,0},{192,64},{1,129},{65,193},{129,1},{193,65... | collective-permute-start | bytes 1572872 | tf_op jit(solution)/shard_map/ppermute | solution.py:337
  103.3 25.1 %collective-permute-start.4 = (bf16[512,512]{1,0:T(8,128)(2,1)S(1)}, bf16[512,512]{1,0:T(8,128)(2,1)S(1)}, u32[]{:S(2)}, u32[]{:S(2)}) collective-permute-start(bf16[512,512]{1,0:T(8,128)(2,1)S(1)} %get-tuple-element.26), channel_id=1, source_target_pairs={{0,192},{64,0},{128,64},{192,128},{1,193},{65,1},{129,65},{193,129... | collective-permute-start | bytes 1572872 | tf_op jit(solution)/shard_map/ppermute | solution.py:337
  128.5 0.8 copy-start.1
  129.3 1.0 copy-start.2
Sparse Core Ops, SparseCore 0:
  9.9 36.2 all-gather.1
